TPU v7x, 512 devices: a whole 4x4x16 slice. The times are simulated.
512 devices in a mesh: rep: 64 (over y_lo, z, core), fsdp: 8 (over y_hi, x).
Axes of the slice: x: 4, y: 4 (y_hi: 2, y_lo: 2; y = y_hi * 2 + y_lo), z: 16, core: 2. Of those that a mesh axis runs over, the one named last changes fastest.
Arguments:
- weights: bfloat16 [64, 4096, 512], P('rep', 'fsdp'), may hold values from -6 to 6
- first_moment: bfloat16 [64, 4096, 512], P('rep', 'fsdp'), may hold values from -4 to 4
- second_moment: bfloat16 [64, 4096, 512], P('rep', 'fsdp'), may hold values from 0.049804688 to 1
- inputs: bfloat16 [64, 1536, 4096], P('rep', 'fsdp'), may hold values from -6 to 6
- cotangent: bfloat16 [64, 1536, 512], P('rep', 'fsdp'), may hold values from -6 to 6
- global_frag: float32 [4096, 128], P(('fsdp', 'rep')), may hold values from -6 to 6
- outer_momentum: bfloat16 [4096, 128], P(('fsdp', 'rep')), may hold values from -6 to 6
- fragment: int32 [4], replicated, may hold values from 0 to 3, each once
- inner_step: int32 [64], P('rep'), may hold values from 1 to 4
Outputs:
- new_weights: bfloat16 [64, 4096, 512], P('rep', 'fsdp')
- new_first: bfloat16 [64, 4096, 512], P('rep', 'fsdp')
- new_second: bfloat16 [64, 4096, 512], P('rep', 'fsdp')
- new_global: float32 [4096, 128], P(('fsdp', 'rep'))
- new_momentum: bfloat16 [4096, 128], P(('fsdp', 'rep'))
Inputs may be any that keep to these rules, and one draw needn't show every extreme that they name: `fragment`: each of 0 to 3 once.
All inputs are finite; a program needn't handle non-finite values.
Results may differ from a plain program's by a relative error of at most 0.0065.
Values may be sent and summed in bfloat16 or wider, within the bound.
A program may use at most 64 MiB of HBM per device.

v0:
```python
import jax
import jax.numpy as jnp
from jax import lax
from jax.sharding import PartitionSpec as P

KVH = 4
HEAD = 128


beta_first = 0.9
beta_second = 0.95
rate_unit = 0.05
weight_decay = 0.1
adam_epsilon = 1e-08
norm_epsilon = 1e-06
outer_rate = 0.7
outer_beta = 0.9
mix_share = 0.5


def column_rates(fragment):
    places = jnp.arange(KVH, dtype=jnp.int32)
    matches = (fragment[:, None] == places[None, :]).astype(jnp.float32)
    positions = jnp.sum(places.astype(jnp.float32)[:, None] * matches, axis=0)
    rates = rate_unit * (1.0 + positions)
    return jnp.repeat(rates, HEAD)


def key_gradient(keys, cotangent_rows):
    token_count = keys.shape[0]
    heads = keys.reshape(token_count, -1, HEAD)
    scale = lax.rsqrt(jnp.mean(heads * heads, axis=-1, keepdims=True) + norm_epsilon)
    normed = heads * scale
    upstream = cotangent_rows.astype(jnp.float32).reshape(heads.shape)
    along = jnp.mean(upstream * normed, axis=-1, keepdims=True)
    return (scale * (upstream - normed * along)).reshape(token_count, -1)


def adam_update(weight_rows, first_rows, second_rows, gradient, step_value, rates):
    first_full = beta_first * first_rows.astype(jnp.float32) + (1.0 - beta_first) * gradient
    second_full = (
        beta_second * second_rows.astype(jnp.float32) + (1.0 - beta_second) * gradient * gradient
    )
    first_hat = first_full / (1.0 - jnp.power(beta_first, step_value))
    second_hat = second_full / (1.0 - jnp.power(beta_second, step_value))
    weight_float = weight_rows.astype(jnp.float32)
    updated = weight_float - rates[None, :] * (
        first_hat / (jnp.sqrt(second_hat) + adam_epsilon) + weight_decay * weight_float
    )
    return (updated, first_full.astype(jnp.bfloat16), second_full.astype(jnp.bfloat16))


def outer_update(global_rows, momentum_rows, average):
    momentum_full = outer_beta * momentum_rows.astype(jnp.float32) + average
    global_new = global_rows - outer_rate * (average + outer_beta * momentum_full)
    return (global_new, momentum_full.astype(jnp.bfloat16))


def mix_fragment(updated, global_new, column_start):
    own_block = lax.dynamic_slice_in_dim(updated, column_start, HEAD, 1)
    blended = mix_share * own_block + (1.0 - mix_share) * global_new
    return lax.dynamic_update_slice_in_dim(updated, blended, column_start, 1)


def local(
    weights,
    first_moment,
    second_moment,
    inputs,
    cotangent,
    global_frag,
    outer_momentum,
    fragment,
    inner_step,
):
    weight_shard = weights[0]
    token_rows = inputs[0]
    cotangent_rows = cotangent[0]
    column_start = fragment[0] * HEAD
    rates = column_rates(fragment)
    step_value = inner_step[0].astype(jnp.float32)
    replica_count = lax.axis_size("rep")
    local_block = lax.dynamic_slice_in_dim(weight_shard, column_start, HEAD, 1).astype(jnp.float32)
    share_rows = global_frag.shape[0]
    summed_all = lax.psum(local_block, "rep")
    share_start = lax.axis_index("rep") * share_rows
    summed = lax.dynamic_slice_in_dim(summed_all, share_start, share_rows, 0)
    average = global_frag - summed / replica_count
    global_part, momentum_new = outer_update(global_frag, outer_momentum, average)
    global_new = lax.all_gather(global_part, "rep", axis=0, tiled=True)
    columns = token_rows
    keys = jnp.dot(
        columns,
        lax.all_gather(weight_shard, "fsdp", axis=0, tiled=True),
        preferred_element_type=jnp.float32,
    )
    key_grad = key_gradient(keys, cotangent_rows).astype(jnp.bfloat16)
    columns = token_rows
    gradient = lax.psum_scatter(
        lax.dot_general(
            columns, key_grad, (((0,), (0,)), ((), ())), preferred_element_type=jnp.float32
        ).astype(jnp.bfloat16),
        "fsdp",
        scatter_dimension=0,
        tiled=True,
    ).astype(jnp.float32)
    updated, first_new, second_new = adam_update(
        weight_shard, first_moment[0], second_moment[0], gradient, step_value, rates
    )
    updated = mix_fragment(updated, global_new, column_start)
    return (
        updated.astype(jnp.bfloat16)[None],
        first_new[None],
        second_new[None],
        global_part,
        momentum_new,
    )


def solution(mesh):
    in_specs = (
        P("rep", "fsdp", None),
        P("rep", "fsdp", None),
        P("rep", "fsdp", None),
        P("rep", "fsdp", None),
        P("rep", "fsdp", None),
        P(("fsdp", "rep"), None),
        P(("fsdp", "rep"), None),
        P(),
        P("rep"),
    )
    out_specs = (
        P("rep", "fsdp", None),
        P("rep", "fsdp", None),
        P("rep", "fsdp", None),
        P(("fsdp", "rep"), None),
        P(("fsdp", "rep"), None),
    )
    return jax.shard_map(local, mesh=mesh, in_specs=in_specs, out_specs=out_specs, check_vma=False)
```

profile of v0, /device:TPU:1, one launch (start us, length us, event | category | flops | bytes accessed | tf_op | source)
XLA Modules:
  0.0 483.6 jit_solution(13569961471275504970)
XLA Ops:
  8.1 0.7 all-gather.3.cloned.1.call-update
  9.4 1.6 bitcast_convert_fusion
  11.2 1.1 reshape.56
  12.2 92.0 %all-gather.3.cloned.1.call-done = bf16[1,4096,512]{2,1,0:T(8,128)(2,1)} async-done(((bf16[1,512,512]{2,1,0:T(8,128)(2,1)}), bf16[1,4096,512]{2,1,0:T(8,128)(2,1)}) %all-gather.3.cloned.1.call-update) | async-done | bytes 4194320 | tf_op jit(solution)/shard_map/all_gather | solution.py:94
  104.2 6.5 %copy.58 = bf16[512,4096]{1,0:T(8,128)(2,1)} copy(bf16[512,4096]{0,1:T(8,128)(2,1)} %bitcast.56) | data formatting | bytes 8388608 | tf_op jit(solution)/shard_map/dot_general | solution.py:92
  110.8 3.9 multiply_reduce_fusion.1
  114.7 0.4 multiply_reduce_fusion
  115.0 3.6 fusion
  118.7 1.0 copy-done.1
  119.7 0.2 copy.56
  119.9 0.2 copy.62
  120.8 1.3 copy.57
  122.1 0.1 select_reduce_fusion
  122.2 0.1 broadcast_bitcast_fusion
  122.3 284.3 %all-reduce.2.cloned.1.call-done = f32[512,128]{1,0:T(8,128)} async-done(((f32[512,128]{1,0:T(8,128)}), f32[512,128]{1,0:T(8,128)}) %all-reduce.2.cloned.1.call-update) | async-done | bytes 262160 | tf_op jit(solution)/shard_map/psum | solution.py:85
  406.6 1.3 fusion.15
  407.9 60.2 %all_gather.7 = f32[512,128]{1,0:T(8,128)S(1)} all-gather(f32[8,128]{1,0:T(8,128)S(1)} %get-tuple-element.29), channel_id=1, replica_groups=mesh['rep'=64,'fsdp'=8] {'rep'}, dimensions={0}, use_global_device_ids=true | all-gather | bytes 266240 | tf_op jit(solution)/shard_map/all_gather | solution.py:90
  468.1 0.8 copy.63
  469.0 3.0 fusion.10
  472.0 0.1 multiply_dynamic-update-slice_fusion
  472.1 0.1 convert_bitcast_fusion
  472.1 1.0 copy.64
  473.1 2.0 copy.65
  475.2 1.0 copy.66
  (27 shorter events, 0.2 us)
Async XLA Ops:
  8.0 102.8 %copy-start = (bf16[1,192,4096]{2,1,0:T(8,128)(2,1)S(1)}, bf16[1,192,4096]{2,1,0:T(8,128)(2,1)}, u32[]{:S(2)}) copy-start(bf16[1,192,4096]{2,1,0:T(8,128)(2,1)} %param.12) | copy-start | bytes 4718596
  8.0 96.2 %all-gather.3.cloned.1.call-start = ((), (), s32[]{:S(2)}) async-start(), calls=%async_computation.3 | async-start | bytes 4718592 | tf_op jit(solution)/shard_map/all_gather | solution.py:94
  8.7 397.9 %all-reduce.2.cloned.1.call-start = ((), (), s32[]{:S(2)}) async-start(), calls=%async_computation.2 | async-start | bytes 524288 | tf_op jit(solution)/shard_map/psum | solution.py:85
  11.1 457.9 %reduce-scatter.2.cloned.1.call-start = ((), (), s32[]{:S(2)}) async-start(), calls=%async_computation.1 | async-start | bytes 4718592 | tf_op jit(solution)/shard_map/reduce_scatter | solution.py:99
  118.6 1.0 copy-start.1
  118.6 1.3 copy-start.4
  118.6 3.5 copy-start.8
  118.6 288.0 %copy-start.6 = (f32[8,128]{1,0:T(8,128)S(1)}, f32[8,128]{1,0:T(8,128)}, u32[]{:S(2)}) copy-start(f32[8,128]{1,0:T(8,128)} %param.14) | copy-start | bytes 12292
  118.6 288.0 %copy-start.7 = (bf16[8,128]{1,0:T(8,128)(2,1)S(1)}, bf16[8,128]{1,0:T(8,128)(2,1)}, u32[]{:S(2)}) copy-start(bf16[8,128]{1,0:T(8,128)(2,1)} %param.15) | copy-start | bytes 6148
  407.9 65.3 %copy-start.5 = (f32[8,128]{1,0:T(8,128)}, f32[8,128]{1,0:T(8,128)S(1)}, u32[]{:S(2)}) copy-start(f32[8,128]{1,0:T(8,128)S(1)} %get-tuple-element.29) | copy-start | bytes 12292
  469.0 3.0 copy-start.3
  472.0 3.2 copy-start.2
Sparse Core Ops, SparseCore 0:
  12.1 92.1 all-gather.2
  118.8 97.5 reduce-scatter.1
Sparse Core Ops, SparseCore 1:
  12.7 393.9 all-reduce.1
where the time goes:
time: 487 us; the launch traced here: 484 us
  waiting for transfers between devices  377 us (77%)
  blocking collectives  60.2 us (12%)
  between operations  17 us (3%)
  local copies, waits for them, and re-layouts  15.2 us (3%)
  matrix products  7.47 us (2%)
  other arithmetic  6.52 us (1%)
    psum x1, waiting for transfers between devices, local(): summed_all = lax.psum(local_block, 'rep')  284 us
    all_gather x1, waiting for transfers between devices, local(): lax.all_gather(weight_shard, 'fsdp', axis=0, tiled=True)  92 us
    all_gather x1, blocking collectives, local(): global_new = lax.all_gather(global_part, 'rep', axis=0, tiled=True)  60.2 us
  transfers between devices with their start and end apart: 3, of which 2 were waited for; matrix products, arithmetic and copies ran while one was open for 4% of the time, Pallas kernels for 0%

commit v1 on v0

v1 whole, which is shorter than its diff:
```python
import functools
import math

import jax
import jax.numpy as jnp
from jax import lax
from jax.experimental import pallas as pl
from jax.experimental.pallas import tpu as pltpu
from jax.sharding import PartitionSpec as P

KVH = 4
HEAD = 128
NX = 4
NY = 2

beta_first = 0.9
beta_second = 0.95
rate_unit = 0.05
weight_decay = 0.1
adam_epsilon = 1e-08
norm_epsilon = 1e-06
outer_rate = 0.7
outer_beta = 0.9
mix_share = 0.5

CHUNKS = 2
MESH = pl.DeviceIdType.MESH
f32 = jnp.float32
bf16 = jnp.bfloat16


def kernel(
    n_rep,
    x_hbm, w_hbm, m_hbm, v_hbm, ct_hbm, gf_ref, om_ref, frag_ref, step_ref,
    nw_hbm, nf_hbm, ns_hbm, ng_ref, nm_ref,
    xall, xt, wall, mv, vv, ct, kown, psend, precv, kgall, gsend, grecv, gown, wout, fout, sout,
    fbuf, fcore, s1, fyl, s2, zrecv, ngall, ng2, ngf,
    lsem, xs, xr, ws, wr, rss, rsr, ags, agr, gs, gr, fs, fr, zs, zr, z2s, z2r, osem, near, far,
):
    nz = n_rep // 4
    tokens = ct.shape[0]
    tok = tokens // CHUNKS
    block = w_hbm.shape[0]
    rep = lax.axis_index("rep")
    me = lax.axis_index("fsdp")
    y, x = me // NX, lax.rem(me, NX)
    core, z, ylo = lax.rem(rep, 2), lax.rem(rep // 2, nz), rep // (2 * nz)
    others = (2, 1, 3)

    def x_peer(o):
        return (rep, y * NX + lax.rem(x + o, NX))

    def z_peer(k):
        return (ylo * 2 * nz + lax.rem(z + k, nz) * 2 + core, me)

    y_peer = (rep, (1 - y) * NX + x)
    core_peer = (rep + 1 - 2 * core, me)
    ylo_peer = ((1 - ylo) * 2 * nz + z * 2 + core, me)

    def remote(src, dst, send, recv, device):
        return pltpu.make_async_remote_copy(
            src_ref=src, dst_ref=dst, send_sem=send, recv_sem=recv,
            device_id=device, device_id_type=MESH,
        )

    def columns(h):
        return pl.ds(h * HEAD, HEAD)

    loads = [
        pltpu.make_async_copy(w_hbm, wall.at[y], lsem.at[0]),
        pltpu.make_async_copy(ct_hbm, ct, lsem.at[1]),
        pltpu.make_async_copy(m_hbm, mv, lsem.at[2]),
        pltpu.make_async_copy(v_hbm, vv, lsem.at[3]),
    ]
    for yy in range(NY):
        start = pl.multiple_of((yy * NX + x) * block, block)
        loads.append(
            pltpu.make_async_copy(
                x_hbm.at[:, pl.ds(start, block)], xall.at[yy, pl.ds(0, tokens)], lsem.at[4 + yy]
            )
        )
    for load in loads:
        load.start()

    near_z = [1, 2, nz - 2, nz - 1] if nz > 4 else []
    peers = [x_peer(o) for o in others] + [y_peer, core_peer, ylo_peer] + [z_peer(k) for k in near_z]
    barrier = pltpu.get_barrier_semaphore()
    for peer in peers:
        pl.semaphore_signal(barrier, inc=1, device_id=peer, device_id_type=MESH)
    pl.semaphore_wait(barrier, len(peers))

    w_copy = remote(w_hbm, wall.at[y], ws.at[0], wr.at[0], y_peer)
    w_copy.start()
    x_copy = {}
    for c in range(CHUNKS):
        for o in others:
            for yy in range(NY):
                start = pl.multiple_of((yy * NX + lax.rem(x + o, NX)) * block, block)
                x_copy[o, c, yy] = remote(
                    x_hbm.at[pl.ds(c * tok, tok), pl.ds(start, block)],
                    xall.at[yy, pl.ds(o * tokens + c * tok, tok)],
                    xs.at[o, c, yy], xr.at[o, c, yy], x_peer(o),
                )
                x_copy[o, c, yy].start()
    if nz > 4:
        for k in near_z:
            pl.semaphore_signal(near, inc=1, device_id=z_peer(k), device_id_type=MESH)

    chosen = [jnp.where(frag_ref[0] == h, 1.0, 0.0) for h in range(KVH)]
    loads[0].wait()
    picked = sum(chosen[h] * wall[y, :, columns(h)].astype(f32) for h in range(KVH))
    fbuf[...] = picked.reshape(fbuf.shape)
    core_copy = remote(fbuf.at[:, :, 1 - core], fcore, fs.at[0], fr.at[0], core_peer)
    core_copy.start()
    core_copy.wait_recv()
    s1[...] = fbuf[:, :, core] + fcore[...]
    ylo_copy = remote(s1.at[1 - ylo], fyl, fs.at[1], fr.at[1], ylo_peer)
    ylo_copy.start()
    if nz > 4:
        pl.semaphore_wait(near, 4)
        for k in (3, 4, nz - 4, nz - 3):
            pl.semaphore_signal(far, inc=1, device_id=z_peer(k), device_id_type=MESH)
    ylo_copy.wait_recv()
    s2[...] = s1[ylo] + fyl[...]
    if nz > 4:
        pl.semaphore_wait(far, 4)

    def z_sum(k):
        return remote(s2.at[lax.rem(z + k, nz)], zrecv.at[k], zs.at[k], zr.at[k], z_peer(k))

    def z_gather(k):
        return remote(ngall.at[z], ngall.at[z], z2s.at[k], z2r.at[k], z_peer(k))

    def each_z(act):
        if nz > 1:
            lax.fori_loop(1, nz, lambda k, carry: (act(k), carry)[1], 0)

    each_z(lambda k: z_sum(k).start())

    rs_copy, ag_copy = {}, {}

    def partial_keys(c, o):
        if o:
            for yy in range(NY):
                x_copy[o, c, yy].wait_recv()
        rows = pl.ds(o * tokens + c * tok, tok)
        for pair in range(KVH // 2):
            wide = pl.ds(pair * 2 * HEAD, 2 * HEAD)
            part = jnp.dot(xall[0, rows, :], wall[0, :, wide], preferred_element_type=f32)
            part += jnp.dot(xall[1, rows, :], wall[1, :, wide], preferred_element_type=f32)
            for i in range(2):
                h = 2 * pair + i
                own = part[:, i * HEAD:(i + 1) * HEAD]
                if o == 0:
                    kown[c, h] = own
                else:
                    psend[o, c, h] = own.astype(bf16)
                    rs_copy[o, c, h] = remote(
                        psend.at[o, c, h], precv.at[o, c, h], rss.at[o, c, h], rsr.at[o, c, h],
                        x_peer(NX - o),
                    )
                    rs_copy[o, c, h].start()

    def key_gradient(c, h):
        keys = kown[c, h]
        for o in others:
            rs_copy[o, c, h].wait_recv()
            keys += precv[o, c, h].astype(f32)
        scale = lax.rsqrt(jnp.mean(keys * keys, axis=-1, keepdims=True) + norm_epsilon)
        normed = keys * scale
        upstream = ct[pl.ds(c * tok, tok), columns(h)].astype(f32)
        along = jnp.mean(upstream * normed, axis=-1, keepdims=True)
        kgall[h, pl.ds(c * tok, tok), :] = (scale * (upstream - normed * along)).astype(bf16)
        for o in others:
            ag_copy[o, c, h] = remote(
                kgall.at[h, pl.ds(c * tok, tok)], kgall.at[h, pl.ds(o * tokens + c * tok, tok)],
                ags.at[o, c, h], agr.at[o, c, h], x_peer(o),
            )
            ag_copy[o, c, h].start()

    w_copy.wait_recv()
    for c in range(CHUNKS):
        if c == CHUNKS - 1:
            each_z(lambda k: z_sum(k).wait_recv())
            total = s2[z]
            if nz > 1:
                total += jnp.sum(zrecv[pl.ds(1, nz - 1)], axis=0)
            average = gf_ref[...] - total / n_rep
            momentum_full = outer_beta * om_ref[...].astype(f32) + average
            global_new = gf_ref[...] - outer_rate * (average + outer_beta * momentum_full)
            ng_ref[...] = global_new
            nm_ref[...] = momentum_full.astype(bf16)
            ngall[z] = global_new
            each_z(lambda k: z_gather(k).start())
        for o in others:
            partial_keys(c, o)
    loads[4].wait()
    loads[5].wait()
    loads[1].wait()
    for c in range(CHUNKS):
        partial_keys(c, 0)
    for c in range(CHUNKS):
        for h in range(KVH):
            key_gradient(c, h)
    for yy in range(NY):
        for piece in range(xall.shape[1] // 256):
            rows = pl.ds(piece * 256, 256)
            xt[yy, :, rows] = xall[yy, rows, :].T

    each_z(lambda k: z_gather(k).wait_recv())
    ylo_back = remote(ngall, ng2.at[ylo], fs.at[2], fr.at[2], ylo_peer)
    ylo_back.start()
    ng2[ylo] = ngall[...]

    g_copy = {}

    def gradient(h):
        for c in range(CHUNKS):
            for o in others:
                ag_copy[o, c, h].wait_recv()
        gsend[h] = jnp.dot(xt[1 - y], kgall[h], preferred_element_type=f32).astype(bf16)
        g_copy[h] = remote(gsend.at[h], grecv.at[h], gs.at[h], gr.at[h], y_peer)
        g_copy[h].start()
        gown[h] = jnp.dot(xt[y], kgall[h], preferred_element_type=f32)

    for h in range(KVH):
        gradient(h)
        if h == 1:
            ylo_back.wait_recv()
            core_back = remote(ng2, ngf.at[:, :, core], fs.at[3], fr.at[3], core_peer)
            core_back.start()
            ngf[:, :, core] = ng2[...]
    core_back.wait_recv()
    loads[2].wait()
    loads[3].wait()

    time = jnp.full((1, HEAD), step_ref[0].astype(f32), f32)
    first_unbias = 1.0 / (1.0 - jnp.exp(time * math.log(beta_first)))
    second_unbias = 1.0 / (1.0 - jnp.exp(time * math.log(beta_second)))
    outs = []
    for h in range(KVH):
        position = sum(jnp.where(frag_ref[j] == h, float(j), 0.0) for j in range(KVH))
        rate = rate_unit * (1.0 + position)
        g_copy[h].wait_recv()
        grad = gown[h] + grecv[h].astype(f32)
        first = beta_first * mv[:, columns(h)].astype(f32) + (1.0 - beta_first) * grad
        second = beta_second * vv[:, columns(h)].astype(f32) + (1.0 - beta_second) * grad * grad
        weight = wall[y, :, columns(h)].astype(f32)
        updated = weight - rate * (
            first * first_unbias / (jnp.sqrt(second * second_unbias) + adam_epsilon)
            + weight_decay * weight
        )
        share = (1.0 - mix_share) * chosen[h]
        updated = (1.0 - share) * updated + share * ngf[...].reshape(block, HEAD)
        wout[h] = updated.astype(bf16)
        fout[h] = first.astype(bf16)
        sout[h] = second.astype(bf16)
        for i, (buf, out) in enumerate(((wout, nw_hbm), (fout, nf_hbm), (sout, ns_hbm))):
            copy = pltpu.make_async_copy(buf.at[h], out.at[:, columns(h)], osem.at[i, h])
            copy.start()
            outs.append(copy)

    for copy in [w_copy, core_copy, ylo_copy, ylo_back, core_back, *g_copy.values()]:
        copy.wait_send()
    for copies in (x_copy, rs_copy, ag_copy):
        for copy in copies.values():
            copy.wait_send()
    each_z(lambda k: z_sum(k).wait_send())
    each_z(lambda k: z_gather(k).wait_send())
    for copy in outs:
        copy.wait()


def solution(mesh):
    n_rep = mesh.shape["rep"]
    nz = n_rep // 4

    def local(weights, first, second, inputs, cotangent, global_frag, outer_momentum, fragment, inner_step):
        block, wide = weights.shape[1:]
        tokens, din = inputs.shape[1:]
        tok = tokens // CHUNKS
        share = global_frag.shape[0]
        any_spec = pl.BlockSpec(memory_space=pl.ANY)
        vmem = pl.BlockSpec(memory_space=pltpu.VMEM)
        smem = pl.BlockSpec(memory_space=pltpu.SMEM)
        dma = pltpu.SemaphoreType.DMA
        results = pl.pallas_call(
            functools.partial(kernel, n_rep),
            out_shape=[jax.ShapeDtypeStruct((block, wide), bf16)] * 3
            + [
                jax.ShapeDtypeStruct(global_frag.shape, f32),
                jax.ShapeDtypeStruct(outer_momentum.shape, bf16),
            ],
            in_specs=[any_spec] * 5 + [vmem] * 2 + [smem] * 2,
            out_specs=[any_spec] * 3 + [vmem] * 2,
            scratch_shapes=[
                pltpu.VMEM((NY, NX * tokens, block), bf16),
                pltpu.VMEM((NY, block, NX * tokens), bf16),
                pltpu.VMEM((NY, block, wide), bf16),
                pltpu.VMEM((block, wide), bf16),
                pltpu.VMEM((block, wide), bf16),
                pltpu.VMEM((tokens, wide), bf16),
                pltpu.VMEM((CHUNKS, KVH, tok, HEAD), f32),
                pltpu.VMEM((NX, CHUNKS, KVH, tok, HEAD), bf16),
                pltpu.VMEM((NX, CHUNKS, KVH, tok, HEAD), bf16),
                pltpu.VMEM((KVH, NX * tokens, HEAD), bf16),
                pltpu.VMEM((KVH, block, HEAD), bf16),
                pltpu.VMEM((KVH, block, HEAD), bf16),
                pltpu.VMEM((KVH, block, HEAD), f32),
                pltpu.VMEM((KVH, block, HEAD), bf16),
                pltpu.VMEM((KVH, block, HEAD), bf16),
                pltpu.VMEM((KVH, block, HEAD), bf16),
                pltpu.VMEM((2, nz, 2, share, HEAD), f32),
                pltpu.VMEM((2, nz, share, HEAD), f32),
                pltpu.VMEM((2, nz, share, HEAD), f32),
                pltpu.VMEM((nz, share, HEAD), f32),
                pltpu.VMEM((nz, share, HEAD), f32),
                pltpu.VMEM((nz, share, HEAD), f32),
                pltpu.VMEM((nz, share, HEAD), f32),
                pltpu.VMEM((2, nz, share, HEAD), f32),
                pltpu.VMEM((2, nz, 2, share, HEAD), f32),
                dma((6,)),
                dma((NX, CHUNKS, NY)), dma((NX, CHUNKS, NY)),
                dma((1,)), dma((1,)),
                dma((NX, CHUNKS, KVH)), dma((NX, CHUNKS, KVH)),
                dma((NX, CHUNKS, KVH)), dma((NX, CHUNKS, KVH)),
                dma((KVH,)), dma((KVH,)),
                dma((4,)), dma((4,)),
                dma((nz,)), dma((nz,)), dma((nz,)), dma((nz,)),
                dma((3, KVH)),
                pltpu.SemaphoreType.REGULAR, pltpu.SemaphoreType.REGULAR,
            ],
            compiler_params=pltpu.CompilerParams(
                collective_id=0, has_side_effects=True, vmem_limit_bytes=48 * 2**20
            ),
        )(
            inputs[0], weights[0], first[0], second[0], cotangent[0],
            global_frag, outer_momentum, fragment, inner_step,
        )
        return (results[0][None], results[1][None], results[2][None], results[3], results[4])

    in_specs = (P("rep", "fsdp", None),) * 5 + (P(("fsdp", "rep"), None),) * 2 + (P(), P("rep"))
    out_specs = (P("rep", "fsdp", None),) * 3 + (P(("fsdp", "rep"), None),) * 2
    return jax.shard_map(local, mesh=mesh, in_specs=in_specs, out_specs=out_specs, check_vma=False)
```

time: 487 us -> 75.3 us (0.15)
  the two profiles are of different devices: /device:TPU:1 before, /device:TPU:24 now
where the time goes in v1:
time: 75.3 us; the launch traced here: 74.9 us
  Pallas kernels  62.6 us (83%)
  local copies, waits for them, and re-layouts  11 us (15%)
  between operations  1.31 us (2%)
    pallas_call x1, Pallas kernels, local(): pl.pallas_call(functools.partial(kernel, n_rep), out_shape=[jax.ShapeDtyp...  62.6 us
    unnamed x21, local copies, waits for them, and re-layouts  11 us

profile of v1, /device:TPU:24, one launch (start us, length us, event | category | flops | bytes accessed | tf_op | source)
XLA Modules:
  0.0 74.9 jit_solution(7305919823047976927)
XLA Ops:
  1.3 0.0 copy-start
  1.3 1.4 %copy-done = bf16[1,192,4096]{2,1,0:T(8,128)(2,1)S(1)} copy-done((bf16[1,192,4096]{2,1,0:T(8,128)(2,1)S(1)}, bf16[1,192,4096]{2,1,0:T(8,128)(2,1)}, u32[]{:S(2)}) %copy-start) | copy-done | bytes 1572888
  2.7 0.0 copy-start.1
  2.7 1.0 %copy-done.1 = bf16[1,512,512]{2,1,0:T(8,128)(2,1)S(1)} copy-done((bf16[1,512,512]{2,1,0:T(8,128)(2,1)S(1)}, bf16[1,512,512]{2,1,0:T(8,128)(2,1)}, u32[]{:S(2)}) %copy-start.1) | copy-done | bytes 524312
  3.7 0.0 copy-start.2
  3.7 1.0 %copy-done.2 = bf16[1,512,512]{2,1,0:T(8,128)(2,1)S(1)} copy-done((bf16[1,512,512]{2,1,0:T(8,128)(2,1)S(1)}, bf16[1,512,512]{2,1,0:T(8,128)(2,1)}, u32[]{:S(2)}) %copy-start.2) | copy-done | bytes 524312
  4.8 0.0 copy-start.3
  4.8 1.0 %copy-done.3 = bf16[1,512,512]{2,1,0:T(8,128)(2,1)S(1)} copy-done((bf16[1,512,512]{2,1,0:T(8,128)(2,1)S(1)}, bf16[1,512,512]{2,1,0:T(8,128)(2,1)}, u32[]{:S(2)}) %copy-start.3) | copy-done | bytes 524312
  5.8 0.0 copy-start.4
  5.8 0.9 %copy-done.4 = bf16[1,192,512]{2,1,0:T(8,128)(2,1)S(1)} copy-done((bf16[1,192,512]{2,1,0:T(8,128)(2,1)S(1)}, bf16[1,192,512]{2,1,0:T(8,128)(2,1)}, u32[]{:S(2)}) %copy-start.4) | copy-done | bytes 196632
  6.7 0.0 copy-start.5
  6.7 0.7 copy-done.5
  7.4 0.0 copy-start.6
  7.4 0.7 copy-done.6
  8.1 0.0 copy-start.7
  8.1 0.7 copy-done.7
  8.8 62.6 %shard_map.128 = (bf16[512,512]{1,0:T(8,128)(2,1)S(1)}, bf16[512,512]{1,0:T(8,128)(2,1)S(1)}, bf16[512,512]{1,0:T(8,128)(2,1)S(1)}, f32[8,128]{1,0:T(8,128)S(1)}, bf16[8,128]{1,0:T(8,128)(2,1)S(1)}) custom-call(bf16[192,4096]{1,0:T(8,128)(2,1)S(1)} %bitcast.8, bf16[512,512]{1,0:T(8,128)(2,1)S(1)} %bitcast.12, bf16[512,512]{1,0:T(8,128)(2,1)S(1)} %bitcast.13, ...), custom_call_target="tpu_custom_call" | custom-call | tf_op jit(solution)/shard_map/pallas_call | solution.py:287
  71.4 0.8 %copy.20 = bf16[1,512,512]{2,1,0:T(8,128)(2,1)} copy(bf16[1,512,512]{2,1,0:T(8,128)(2,1)S(1)} %bitcast.11) | data formatting | bytes 1048576
  72.2 0.8 %copy.21 = bf16[1,512,512]{2,1,0:T(8,128)(2,1)} copy(bf16[1,512,512]{2,1,0:T(8,128)(2,1)S(1)} %bitcast.10) | data formatting | bytes 1048576
  73.0 0.8 %copy.22 = bf16[1,512,512]{2,1,0:T(8,128)(2,1)} copy(bf16[1,512,512]{2,1,0:T(8,128)(2,1)S(1)} %bitcast.9) | data formatting | bytes 1048576
  73.8 0.6 copy.23
  74.4 0.6 copy.24
Async XLA Ops:
  1.3 1.4 %copy-start = (bf16[1,192,4096]{2,1,0:T(8,128)(2,1)S(1)}, bf16[1,192,4096]{2,1,0:T(8,128)(2,1)}, u32[]{:S(2)}) copy-start(bf16[1,192,4096]{2,1,0:T(8,128)(2,1)} %param.12) | copy-start | bytes 4718596
  2.7 1.0 %copy-start.1 = (bf16[1,512,512]{2,1,0:T(8,128)(2,1)S(1)}, bf16[1,512,512]{2,1,0:T(8,128)(2,1)}, u32[]{:S(2)}) copy-start(bf16[1,512,512]{2,1,0:T(8,128)(2,1)} %param.9) | copy-start | bytes 1572868
  3.7 1.0 %copy-start.2 = (bf16[1,512,512]{2,1,0:T(8,128)(2,1)S(1)}, bf16[1,512,512]{2,1,0:T(8,128)(2,1)}, u32[]{:S(2)}) copy-start(bf16[1,512,512]{2,1,0:T(8,128)(2,1)} %param.10) | copy-start | bytes 1572868
  4.8 1.0 %copy-start.3 = (bf16[1,512,512]{2,1,0:T(8,128)(2,1)S(1)}, bf16[1,512,512]{2,1,0:T(8,128)(2,1)}, u32[]{:S(2)}) copy-start(bf16[1,512,512]{2,1,0:T(8,128)(2,1)} %param.11) | copy-start | bytes 1572868
  5.8 0.9 %copy-start.4 = (bf16[1,192,512]{2,1,0:T(8,128)(2,1)S(1)}, bf16[1,192,512]{2,1,0:T(8,128)(2,1)}, u32[]{:S(2)}) copy-start(bf16[1,192,512]{2,1,0:T(8,128)(2,1)} %param.13) | copy-start | bytes 589828
  6.7 0.7 copy-start.5
  7.4 0.7 copy-start.6
  8.1 0.7 copy-start.7

commit v2 on v1

v2 whole, which is shorter than its diff:
```python
import functools
import math

import jax
import jax.numpy as jnp
from jax import lax
from jax.experimental import pallas as pl
from jax.experimental.pallas import tpu as pltpu
from jax.sharding import PartitionSpec as P

KVH = 4
HEAD = 128
NX = 4
NY = 2

beta_first = 0.9
beta_second = 0.95
rate_unit = 0.05
weight_decay = 0.1
adam_epsilon = 1e-08
norm_epsilon = 1e-06
outer_rate = 0.7
outer_beta = 0.9
mix_share = 0.5

PIECES = (192,)
ORDER = (
    "P00", "R00", "R01", "P01", "R02", "R03", "ZS", "XT", "K00", "K01", "K02", "K03", "G0", "G1", "YB",
    "G2", "G3", "CB", "M0", "M1", "M2", "M3", "A0", "A1", "A2", "A3",
)
MESH = pl.DeviceIdType.MESH
f32 = jnp.float32
bf16 = jnp.bfloat16


def kernel(
    n_rep,
    x_hbm, w_hbm, m_hbm, v_hbm, ct_hbm, gf_hbm, om_hbm, frag_hbm, step_hbm,
    nw_hbm, nf_hbm, ns_hbm, ng_hbm, nm_hbm,
    xall, xt, wall, mv, vv, ct, kown, psend, precv, kgall, gsend, grecv, gown, wout, fout, sout,
    gf_ref, om_ref, ng_ref, nm_ref, frag_ref, step_ref, fbuf, fcore, s1, fyl, s2, zrecv, ngall, ng2, ngf,
    lsem, xs, xr, ws, wr, rss, rsr, ags, agr, gs, gr, fs, fr, zs, zr, z2s, z2r, osem, near, near_z, mid, far,
):
    nz = n_rep // 4
    tokens = ct.shape[0]
    pieces = [(sum(PIECES[:c]), size) for c, size in enumerate(PIECES)]
    block = w_hbm.shape[0]
    rep = lax.axis_index("rep")
    me = lax.axis_index("fsdp")
    y, x = me // NX, lax.rem(me, NX)
    core, z, ylo = lax.rem(rep, 2), lax.rem(rep // 2, nz), rep // (2 * nz)
    others = (2, 1, 3)

    def x_peer(o):
        return (rep, y * NX + lax.rem(x + o, NX))

    def z_peer(k):
        return (ylo * 2 * nz + lax.rem(z + k, nz) * 2 + core, me)

    y_peer = (rep, (1 - y) * NX + x)
    core_peer = (rep + 1 - 2 * core, me)
    ylo_peer = ((1 - ylo) * 2 * nz + z * 2 + core, me)

    def remote(src, dst, send, recv, device):
        return pltpu.make_async_remote_copy(
            src_ref=src, dst_ref=dst, send_sem=send, recv_sem=recv,
            device_id=device, device_id_type=MESH,
        )

    def columns(h):
        return pl.ds(h * HEAD, HEAD)

    loads = [
        pltpu.make_async_copy(w_hbm, wall.at[y], lsem.at[0]),
        pltpu.make_async_copy(ct_hbm, ct, lsem.at[1]),
        pltpu.make_async_copy(m_hbm, mv, lsem.at[2]),
        pltpu.make_async_copy(v_hbm, vv, lsem.at[3]),
    ]
    for yy in range(NY):
        start = pl.multiple_of((yy * NX + x) * block, block)
        loads.append(
            pltpu.make_async_copy(
                x_hbm.at[:, pl.ds(start, block)], xall.at[yy, pl.ds(0, tokens)], lsem.at[4 + yy]
            )
        )
    loads += [
        pltpu.make_async_copy(frag_hbm, frag_ref, lsem.at[6]),
        pltpu.make_async_copy(step_hbm, step_ref, lsem.at[7]),
        pltpu.make_async_copy(gf_hbm, gf_ref, lsem.at[8]),
        pltpu.make_async_copy(om_hbm, om_ref, lsem.at[9]),
    ]
    for load in loads:
        load.start()

    def y_near(step):
        place = lax.rem(NY * y + ylo + step, 4)
        return (lax.rem(place, 2) * 2 * nz + z * 2 + core, place // 2 * NX + x)

    def x_send(c, o):
        first, size = pieces[c]
        for yy in range(NY):
            start = pl.multiple_of((yy * NX + lax.rem(x + o, NX)) * block, block)
            x_copy[o, c, yy] = remote(
                x_hbm.at[pl.ds(first, size), pl.ds(start, block)],
                xall.at[yy, pl.ds(o * tokens + first, size)],
                xs.at[o, c, yy], xr.at[o, c, yy], x_peer(o),
            )
            x_copy[o, c, yy].start()

    def tell(semaphore, devices):
        for device in devices:
            pl.semaphore_signal(semaphore, inc=1, device_id=device, device_id_type=MESH)

    around = [x_peer(1), x_peer(3), y_near(1), y_near(3)]
    barrier = pltpu.get_barrier_semaphore()
    tell(barrier, around + [core_peer])
    if nz > 1:
        z_near = [z_peer(1), z_peer(nz - 1)]

        @pl.when(z == 0)
        def _():
            pl.semaphore_wait(barrier, len(around) + 1)
            tell(barrier, z_near)

        @pl.when(z != 0)
        def _():
            @pl.when(z != nz - 1)
            def _():
                tell(barrier, z_near[:1])

            @pl.when(z != 1)
            def _():
                tell(barrier, z_near[1:])

            pl.semaphore_wait(barrier, len(around) + 3)

            @pl.when(z == nz - 1)
            def _():
                tell(barrier, z_near[:1])

            @pl.when(z == 1)
            def _():
                tell(barrier, z_near[1:])
    else:
        pl.semaphore_wait(barrier, len(around) + 1)
    tell(near, around)
    x_copy = {}
    x_send(0, 1)
    x_send(0, 3)
    pl.semaphore_wait(near, len(around))
    x_send(0, 2)
    w_copy = remote(w_hbm, wall.at[y], ws.at[0], wr.at[0], y_peer)
    w_copy.start()
    for c in range(1, len(pieces)):
        for o in others:
            x_send(c, o)

    loads[0].wait()
    loads[6].wait()
    chosen = [jnp.where(frag_ref[0] == h, 1.0, 0.0) for h in range(KVH)]
    picked = sum(chosen[h] * wall[y, :, columns(h)].astype(f32) for h in range(KVH))
    fbuf[...] = picked.reshape(fbuf.shape)
    core_copy = remote(fbuf.at[:, :, 1 - core], fcore, fs.at[0], fr.at[0], core_peer)
    core_copy.start()
    core_copy.wait_recv()
    s1[...] = fbuf[:, :, core] + fcore[...]
    ylo_copy = remote(s1.at[1 - ylo], fyl, fs.at[1], fr.at[1], ylo_peer)
    ylo_copy.start()
    if nz > 1:
        @pl.when(z == 0)
        def _():
            pl.semaphore_wait(barrier, 2)

        tell(near_z, z_near)
        pl.semaphore_wait(near_z, 2)
        tell(mid, [z_peer(2), z_peer(nz - 2)])
        pl.semaphore_wait(mid, 2)
        tell(far, [z_peer(k) for k in (3, 4, nz - 4, nz - 3)])
    ylo_copy.wait_recv()
    s2[...] = s1[ylo] + fyl[...]
    if nz > 1:
        pl.semaphore_wait(far, 4)

    def z_sum(k):
        return remote(s2.at[lax.rem(z + k, nz)], zrecv.at[k], zs.at[k], zr.at[k], z_peer(k))

    def z_gather(k):
        return remote(ngall.at[z], ngall.at[z], z2s.at[k], z2r.at[k], z_peer(k))

    def each_z(act):
        if nz > 1:
            lax.fori_loop(1, nz, lambda k, carry: (act(k), carry)[1], 0)

    each_z(lambda k: z_sum(k).start())

    rs_copy, ag_copy, g_copy, outs, back = {}, {}, {}, [], []
    arrived = set()

    def partial_keys(c, pair):
        first, size = pieces[c]
        wide = pl.ds(pair * 2 * HEAD, 2 * HEAD)
        for o in (1, 3, 2, 0):
            if (c, o) not in arrived:
                arrived.add((c, o))
                for yy in range(NY):
                    if o:
                        x_copy[o, c, yy].wait_recv()
                    elif c == 0:
                        loads[4 + yy].wait()
            rows = pl.ds(o * tokens + first, size)
            part = jnp.dot(xall[0, rows, :], wall[0, :, wide], preferred_element_type=f32)
            part += jnp.dot(xall[1, rows, :], wall[1, :, wide], preferred_element_type=f32)
            for i in range(2):
                own = part[:, i * HEAD:(i + 1) * HEAD]
                if o == 0:
                    kown[2 * pair + i, pl.ds(first, size)] = own
                else:
                    psend[o, 2 * pair + i, pl.ds(first, size)] = own.astype(bf16)

    def send_partial(c, h):
        first, size = pieces[c]
        for o in others:
            at = (o, h, pl.ds(first, size))
            rs_copy[o, c, h] = remote(
                psend.at[at], precv.at[at], rss.at[o, c, h], rsr.at[o, c, h], x_peer(NX - o)
            )
            rs_copy[o, c, h].start()

    def key_gradient(c, h):
        first, size = pieces[c]
        rows = pl.ds(first, size)
        keys = kown[h, rows]
        for o in others:
            rs_copy[o, c, h].wait_recv()
            keys += precv[o, h, rows].astype(f32)
        scale = lax.rsqrt(jnp.mean(keys * keys, axis=-1, keepdims=True) + norm_epsilon)
        normed = keys * scale
        upstream = ct[rows, columns(h)].astype(f32)
        along = jnp.mean(upstream * normed, axis=-1, keepdims=True)
        kgall[h, rows, :] = (scale * (upstream - normed * along)).astype(bf16)
        for o in others:
            ag_copy[o, c, h] = remote(
                kgall.at[h, rows], kgall.at[h, pl.ds(o * tokens + first, size)],
                ags.at[o, c, h], agr.at[o, c, h], x_peer(o),
            )
            ag_copy[o, c, h].start()

    def turn():
        for yy in range(NY):
            for piece in range(xall.shape[1] // 256):
                rows = pl.ds(piece * 256, 256)
                xt[yy, :, rows] = xall[yy, rows, :].T

    def send_gradient(h):
        for c in range(len(pieces)):
            for o in others:
                ag_copy[o, c, h].wait_recv()
        gsend[h] = jnp.dot(xt[1 - y], kgall[h], preferred_element_type=f32).astype(bf16)
        g_copy[h] = remote(gsend.at[h], grecv.at[h], gs.at[h], gr.at[h], y_peer)
        g_copy[h].start()

    def own_gradient(h):
        gown[h] = jnp.dot(xt[y], kgall[h], preferred_element_type=f32)

    def outer_update():
        each_z(lambda k: z_sum(k).wait_recv())
        total = s2[z]
        if nz > 1:
            total += jnp.sum(zrecv[pl.ds(1, nz - 1)], axis=0)
        loads[8].wait()
        loads[9].wait()
        average = gf_ref[...] - total / n_rep
        momentum_full = outer_beta * om_ref[...].astype(f32) + average
        global_new = gf_ref[...] - outer_rate * (average + outer_beta * momentum_full)
        ngall[z] = global_new
        each_z(lambda k: z_gather(k).start())
        ng_ref[...] = global_new
        nm_ref[...] = momentum_full.astype(bf16)
        outs.append(pltpu.make_async_copy(ng_ref, ng_hbm, lsem.at[10]))
        outs.append(pltpu.make_async_copy(nm_ref, nm_hbm, lsem.at[11]))
        for copy in outs:
            copy.start()

    def ylo_return():
        each_z(lambda k: z_gather(k).wait_recv())
        back.append(remote(ngall, ng2.at[ylo], fs.at[2], fr.at[2], ylo_peer))
        back[0].start()
        ng2[ylo] = ngall[...]

    def core_return():
        back[0].wait_recv()
        back.append(remote(ng2, ngf.at[:, :, core], fs.at[3], fr.at[3], core_peer))
        back[1].start()
        ngf[:, :, core] = ng2[...]

    def adam(h):
        if h == 0:
            back[1].wait_recv()
            loads[2].wait()
            loads[3].wait()
        time = jnp.full((1, HEAD), step_ref[0].astype(f32), f32)
        first_unbias = 1.0 / (1.0 - jnp.exp(time * math.log(beta_first)))
        second_unbias = 1.0 / (1.0 - jnp.exp(time * math.log(beta_second)))
        position = sum(jnp.where(frag_ref[j] == h, float(j), 0.0) for j in range(KVH))
        rate = rate_unit * (1.0 + position)
        g_copy[h].wait_recv()
        grad = gown[h] + grecv[h].astype(f32)
        first = beta_first * mv[:, columns(h)].astype(f32) + (1.0 - beta_first) * grad
        second = beta_second * vv[:, columns(h)].astype(f32) + (1.0 - beta_second) * grad * grad
        weight = wall[y, :, columns(h)].astype(f32)
        updated = weight - rate * (
            first * first_unbias / (jnp.sqrt(second * second_unbias) + adam_epsilon)
            + weight_decay * weight
        )
        share = (1.0 - mix_share) * chosen[h]
        updated = (1.0 - share) * updated + share * ngf[...].reshape(block, HEAD)
        wout[h] = updated.astype(bf16)
        fout[h] = first.astype(bf16)
        sout[h] = second.astype(bf16)
        for i, (buf, out) in enumerate(((wout, nw_hbm), (fout, nf_hbm), (sout, ns_hbm))):
            copy = pltpu.make_async_copy(buf.at[h], out.at[:, columns(h)], osem.at[i, h])
            copy.start()
            outs.append(copy)

    w_copy.wait_recv()
    loads[1].wait()
    loads[7].wait()
    steps = {
        "P": partial_keys, "R": send_partial, "K": key_gradient, "XT": turn, "G": send_gradient, "M": own_gradient,
        "ZS": outer_update, "YB": ylo_return, "CB": core_return, "A": adam,
    }
    for name in ORDER:
        if name in steps:
            steps[name]()
        else:
            steps[name[0]](*map(int, name[1:]))

    for copy in [w_copy, core_copy, ylo_copy, *back, *g_copy.values()]:
        copy.wait_send()
    for copies in (x_copy, rs_copy, ag_copy):
        for copy in copies.values():
            copy.wait_send()
    each_z(lambda k: z_sum(k).wait_send())
    each_z(lambda k: z_gather(k).wait_send())
    for copy in outs:
        copy.wait()


def writer(*refs):
    sources, targets, held, sems = refs[:5], refs[5:10], refs[10:15], refs[15]
    loads = [pltpu.make_async_copy(a, b, sems.at[0, i]) for i, (a, b) in enumerate(zip(sources, held))]
    stores = [pltpu.make_async_copy(a, b, sems.at[1, i]) for i, (a, b) in enumerate(zip(held, targets))]
    for load in loads:
        load.start()
    for load, store in zip(loads, stores):
        load.wait()
        store.start()
    for store in stores:
        store.wait()


def solution(mesh):
    n_rep = mesh.shape["rep"]
    nz = n_rep // 4

    def local(weights, first, second, inputs, cotangent, global_frag, outer_momentum, fragment, inner_step):
        block, wide = weights.shape[1:]
        tokens, din = inputs.shape[1:]
        share = global_frag.shape[0]
        hbm = pl.BlockSpec(memory_space=pltpu.HBM)
        dma = pltpu.SemaphoreType.DMA
        results = pl.pallas_call(
            functools.partial(kernel, n_rep),
            out_shape=[jax.ShapeDtypeStruct((block, wide), bf16)] * 3
            + [
                jax.ShapeDtypeStruct(global_frag.shape, f32),
                jax.ShapeDtypeStruct(outer_momentum.shape, bf16),
            ],
            in_specs=[hbm] * 9,
            out_specs=[hbm] * 5,
            scratch_shapes=[
                pltpu.VMEM((NY, NX * tokens, block), bf16),
                pltpu.VMEM((NY, block, NX * tokens), bf16),
                pltpu.VMEM((NY, block, wide), bf16),
                pltpu.VMEM((block, wide), bf16),
                pltpu.VMEM((block, wide), bf16),
                pltpu.VMEM((tokens, wide), bf16),
                pltpu.VMEM((KVH, tokens, HEAD), f32),
                pltpu.VMEM((NX, KVH, tokens, HEAD), bf16),
                pltpu.VMEM((NX, KVH, tokens, HEAD), bf16),
                pltpu.VMEM((KVH, NX * tokens, HEAD), bf16),
                pltpu.VMEM((KVH, block, HEAD), bf16),
                pltpu.VMEM((KVH, block, HEAD), bf16),
                pltpu.VMEM((KVH, block, HEAD), f32),
                pltpu.VMEM((KVH, block, HEAD), bf16),
                pltpu.VMEM((KVH, block, HEAD), bf16),
                pltpu.VMEM((KVH, block, HEAD), bf16),
                pltpu.VMEM(global_frag.shape, f32),
                pltpu.VMEM(outer_momentum.shape, bf16),
                pltpu.VMEM(global_frag.shape, f32),
                pltpu.VMEM(outer_momentum.shape, bf16),
                pltpu.SMEM(fragment.shape, jnp.int32),
                pltpu.SMEM(inner_step.shape, jnp.int32),
                pltpu.VMEM((2, nz, 2, share, HEAD), f32),
                pltpu.VMEM((2, nz, share, HEAD), f32),
                pltpu.VMEM((2, nz, share, HEAD), f32),
                pltpu.VMEM((nz, share, HEAD), f32),
                pltpu.VMEM((nz, share, HEAD), f32),
                pltpu.VMEM((nz, share, HEAD), f32),
                pltpu.VMEM((nz, share, HEAD), f32),
                pltpu.VMEM((2, nz, share, HEAD), f32),
                pltpu.VMEM((2, nz, 2, share, HEAD), f32),
                dma((12,)),
                dma((NX, len(PIECES), NY)), dma((NX, len(PIECES), NY)),
                dma((1,)), dma((1,)),
                dma((NX, len(PIECES), KVH)), dma((NX, len(PIECES), KVH)),
                dma((NX, len(PIECES), KVH)), dma((NX, len(PIECES), KVH)),
                dma((KVH,)), dma((KVH,)),
                dma((4,)), dma((4,)),
                dma((nz,)), dma((nz,)), dma((nz,)), dma((nz,)),
                dma((3, KVH)),
                *[pltpu.SemaphoreType.REGULAR] * 4,
            ],
            compiler_params=pltpu.CompilerParams(
                collective_id=0, has_side_effects=True, vmem_limit_bytes=60 * 2**20
            ),
        )(
            inputs[0], weights[0], first[0], second[0], cotangent[0],
            global_frag, outer_momentum, fragment, inner_step,
        )
        results = pl.pallas_call(
            writer,
            out_shape=[jax.ShapeDtypeStruct(r.shape, r.dtype) for r in results],
            in_specs=[hbm] * 5,
            out_specs=[hbm] * 5,
            scratch_shapes=[*[pltpu.VMEM(r.shape, r.dtype) for r in results], dma((2, 5))],
            compiler_params=pltpu.CompilerParams(vmem_limit_bytes=60 * 2**20),
        )(*results)
        return (results[0][None], results[1][None], results[2][None], results[3], results[4])

    in_specs = (P("rep", "fsdp", None),) * 5 + (P(("fsdp", "rep"), None),) * 2 + (P(), P("rep"))
    out_specs = (P("rep", "fsdp", None),) * 3 + (P(("fsdp", "rep"), None),) * 2
    return jax.shard_map(local, mesh=mesh, in_specs=in_specs, out_specs=out_specs, check_vma=False)
```

time: 75.3 us -> 61.3 us (0.81)
  the two profiles are of different devices: /device:TPU:24 before, /device:TPU:1 now
where the time goes in v2:
time: 61.3 us; the launch traced here: 60.5 us
  Pallas kernels  59.2 us (97%)
  between operations  1.29 us (2%)
    pallas_call x1, Pallas kernels, local(): pl.pallas_call(functools.partial(kernel, n_rep), out_shape=[jax.ShapeDtyp...  56.9 us
    pallas_call x1, Pallas kernels, local(): pl.pallas_call(writer, out_shape=[jax.ShapeDtypeStruct(r.shape, r.dtype)...  2.27 us

profile of v2, /device:TPU:1, one launch (start us, length us, event | category | flops | bytes accessed | tf_op | source)
XLA Modules:
  0.0 60.5 jit_solution(13172725739223262379)
XLA Ops:
  1.3 56.9 %shard_map.128 = (bf16[512,512]{1,0:T(8,128)(2,1)}, bf16[512,512]{1,0:T(8,128)(2,1)}, bf16[512,512]{1,0:T(8,128)(2,1)}, f32[8,128]{1,0:T(8,128)}, bf16[8,128]{1,0:T(8,128)(2,1)}) custom-call(bf16[192,4096]{1,0:T(8,128)(2,1)} %bitcast.8, bf16[512,512]{1,0:T(8,128)(2,1)} %bitcast.9, bf16[512,512]{1,0:T(8,128)(2,1)} %bitcast.10, bf16[512,512]{1,0:T(8,128)(2,1)} %bitcast.11, ...), custom_call_target="tpu_custom_call" | custom-call | tf_op jit(solution)/shard_map/pallas_call | solution.py:372
  58.2 2.3 %shard_map.129 = (bf16[512,512]{1,0:T(8,128)(2,1)}, bf16[512,512]{1,0:T(8,128)(2,1)}, bf16[512,512]{1,0:T(8,128)(2,1)}, f32[8,128]{1,0:T(8,128)}, bf16[8,128]{1,0:T(8,128)(2,1)}) custom-call(bf16[512,512]{1,0:T(8,128)(2,1)} %get-tuple-element.15.refs_0_, bf16[512,512]{1,0:T(8,128)(2,1)} %get-tuple-element.16.refs_1_, ...), custom_call_target="tpu_custom_call" | custom-call | tf_op jit(solution)/shard_map/pallas_call | solution.py:431

commit v3 on v2

--- a/solution.py
+++ b/solution.py
@@ -25,8 +25,8 @@
 
 PIECES = (192,)
 ORDER = (
-    "P00", "R00", "R01", "P01", "R02", "R03", "ZS", "XT", "K00", "K01", "K02", "K03", "G0", "G1", "YB",
-    "G2", "G3", "CB", "M0", "M1", "M2", "M3", "A0", "A1", "A2", "A3",
+    "P00", "R00", "R01", "P01", "R02", "R03", "Z0", "XT", "K00", "K01", "Z1", "K02", "K03", "G0", "YB",
+    "G1", "G2", "G3", "M0", "M1", "CB", "M2", "M3", "L", "A0", "A1", "A2", "A3",
 )
 MESH = pl.DeviceIdType.MESH
 f32 = jnp.float32
@@ -147,6 +147,11 @@
     x_copy = {}
     x_send(0, 1)
     x_send(0, 3)
+    if nz > 1:
+        @pl.when(z != 0)
+        def _():
+            tell(near_z, z_near)
+
     pl.semaphore_wait(near, len(around))
     x_send(0, 2)
     w_copy = remote(w_hbm, wall.at[y], ws.at[0], wr.at[0], y_peer)
@@ -170,8 +175,8 @@
         @pl.when(z == 0)
         def _():
             pl.semaphore_wait(barrier, 2)
-
-        tell(near_z, z_near)
+            tell(near_z, z_near)
+
         pl.semaphore_wait(near_z, 2)
         tell(mid, [z_peer(2), z_peer(nz - 2)])
         pl.semaphore_wait(mid, 2)
@@ -193,7 +198,11 @@
 
     each_z(lambda k: z_sum(k).start())
 
-    rs_copy, ag_copy, g_copy, outs, back = {}, {}, {}, [], []
+    rs_copy, ag_copy, g_copy, back = {}, {}, {}, []
+    outs = [
+        pltpu.make_async_copy(ng_ref, ng_hbm, lsem.at[10]),
+        pltpu.make_async_copy(nm_ref, nm_hbm, lsem.at[11]),
+    ]
     arrived = set()
 
     def partial_keys(c, pair):
@@ -262,7 +271,13 @@
     def own_gradient(h):
         gown[h] = jnp.dot(xt[y], kgall[h], preferred_element_type=f32)
 
-    def outer_update():
+    def outer_update(first_plane):
+        if nz > 1:
+            pl.when(z == 0 if first_plane else z != 0)(outer_rows)
+        elif first_plane:
+            outer_rows()
+
+    def outer_rows():
         each_z(lambda k: z_sum(k).wait_recv())
         total = s2[z]
         if nz > 1:
@@ -276,8 +291,6 @@
         each_z(lambda k: z_gather(k).start())
         ng_ref[...] = global_new
         nm_ref[...] = momentum_full.astype(bf16)
-        outs.append(pltpu.make_async_copy(ng_ref, ng_hbm, lsem.at[10]))
-        outs.append(pltpu.make_async_copy(nm_ref, nm_hbm, lsem.at[11]))
         for copy in outs:
             copy.start()
 
@@ -292,6 +305,15 @@
         back.append(remote(ng2, ngf.at[:, :, core], fs.at[3], fr.at[3], core_peer))
         back[1].start()
         ngf[:, :, core] = ng2[...]
+
+    def all_left():
+        for copy in [w_copy, core_copy, ylo_copy, back[0]]:
+            copy.wait_send()
+        for copies in (x_copy, rs_copy, ag_copy):
+            for copy in copies.values():
+                copy.wait_send()
+        each_z(lambda k: z_sum(k).wait_send())
+        each_z(lambda k: z_gather(k).wait_send())
 
     def adam(h):
         if h == 0:
@@ -327,7 +349,7 @@
     loads[7].wait()
     steps = {
         "P": partial_keys, "R": send_partial, "K": key_gradient, "XT": turn, "G": send_gradient, "M": own_gradient,
-        "ZS": outer_update, "YB": ylo_return, "CB": core_return, "A": adam,
+        "Z": outer_update, "YB": ylo_return, "CB": core_return, "L": all_left, "A": adam,
     }
     for name in ORDER:
         if name in steps:
@@ -335,13 +357,8 @@
         else:
             steps[name[0]](*map(int, name[1:]))
 
-    for copy in [w_copy, core_copy, ylo_copy, *back, *g_copy.values()]:
+    for copy in [back[1], *g_copy.values()]:
         copy.wait_send()
-    for copies in (x_copy, rs_copy, ag_copy):
-        for copy in copies.values():
-            copy.wait_send()
-    each_z(lambda k: z_sum(k).wait_send())
-    each_z(lambda k: z_gather(k).wait_send())
     for copy in outs:
         copy.wait()
 

time: 61.3 us -> 60.9 us (level)
  the two profiles are of different devices: /device:TPU:1 before, /device:TPU:16 now
where the time goes in v3:
time: 60.9 us; the launch traced here: 60.8 us
  Pallas kernels  59.5 us (98%)
  between operations  1.29 us (2%)
    pallas_call x1, Pallas kernels, local(): pl.pallas_call(functools.partial(kernel, n_rep), out_shape=[jax.ShapeDtyp...  57.2 us
    pallas_call x1, Pallas kernels, local(): pl.pallas_call(writer, out_shape=[jax.ShapeDtypeStruct(r.shape, r.dtype)...  2.27 us

profile of v3, /device:TPU:16, one launch (start us, length us, event | category | flops | bytes accessed | tf_op | source)
XLA Modules:
  0.0 60.8 jit_solution(8009822330597069191)
XLA Ops:
  1.3 57.2 %shard_map.128 = (bf16[512,512]{1,0:T(8,128)(2,1)}, bf16[512,512]{1,0:T(8,128)(2,1)}, bf16[512,512]{1,0:T(8,128)(2,1)}, f32[8,128]{1,0:T(8,128)}, bf16[8,128]{1,0:T(8,128)(2,1)}) custom-call(bf16[192,4096]{1,0:T(8,128)(2,1)} %bitcast.8, bf16[512,512]{1,0:T(8,128)(2,1)} %bitcast.9, bf16[512,512]{1,0:T(8,128)(2,1)} %bitcast.10, bf16[512,512]{1,0:T(8,128)(2,1)} %bitcast.11, ...), custom_call_target="tpu_custom_call" | custom-call | tf_op jit(solution)/shard_map/pallas_call | solution.py:389
  58.5 2.3 %shard_map.129 = (bf16[512,512]{1,0:T(8,128)(2,1)}, bf16[512,512]{1,0:T(8,128)(2,1)}, bf16[512,512]{1,0:T(8,128)(2,1)}, f32[8,128]{1,0:T(8,128)}, bf16[8,128]{1,0:T(8,128)(2,1)}) custom-call(bf16[512,512]{1,0:T(8,128)(2,1)} %get-tuple-element.15.refs_0_, bf16[512,512]{1,0:T(8,128)(2,1)} %get-tuple-element.16.refs_1_, ...), custom_call_target="tpu_custom_call" | custom-call | tf_op jit(solution)/shard_map/pallas_call | solution.py:448

commit v4 on v3

--- a/solution.py
+++ b/solution.py
@@ -25,8 +25,8 @@
 
 PIECES = (192,)
 ORDER = (
-    "P00", "R00", "R01", "P01", "R02", "R03", "Z0", "XT", "K00", "K01", "Z1", "K02", "K03", "G0", "YB",
-    "G1", "G2", "G3", "M0", "M1", "CB", "M2", "M3", "L", "A0", "A1", "A2", "A3",
+    "P00", "R00", "T1", "P01", "T2", "T3", "Z0", "XT", "B0", "K00", "F1", "F2", "F3", "K01", "Z1", "K02",
+    "K03", "B1", "G0", "G1", "G2", "G3", "M0", "M1", "CB", "M2", "M3", "L", "A0", "A1", "A2", "A3",
 )
 MESH = pl.DeviceIdType.MESH
 f32 = jnp.float32
@@ -38,8 +38,8 @@
     x_hbm, w_hbm, m_hbm, v_hbm, ct_hbm, gf_hbm, om_hbm, frag_hbm, step_hbm,
     nw_hbm, nf_hbm, ns_hbm, ng_hbm, nm_hbm,
     xall, xt, wall, mv, vv, ct, kown, psend, precv, kgall, gsend, grecv, gown, wout, fout, sout,
-    gf_ref, om_ref, ng_ref, nm_ref, frag_ref, step_ref, fbuf, fcore, s1, fyl, s2, zrecv, ngall, ng2, ngf,
-    lsem, xs, xr, ws, wr, rss, rsr, ags, agr, gs, gr, fs, fr, zs, zr, z2s, z2r, osem, near, near_z, mid, far,
+    gf_ref, om_ref, ng_ref, nm_ref, frag_ref, step_ref, fbuf, fcore, s1, fyl, s2, zrecv, ngall, ngf,
+    lsem, xs, xr, ws, wr, rss, rsr, ags, agr, gs, gr, fs, fr, zs, zr, z2s, z2r, osem, near, near_z, mid, far, held, hs, hr,
 ):
     nz = n_rep // 4
     tokens = ct.shape[0]
@@ -198,7 +198,9 @@
 
     each_z(lambda k: z_sum(k).start())
 
-    rs_copy, ag_copy, g_copy, back = {}, {}, {}, []
+    rs_copy, ag_copy, g_copy = {}, {}, {}
+    ylo_back = remote(ngall.at[z, ylo], ngall.at[z, ylo], fs.at[2], fr.at[2], ylo_peer)
+    core_back = remote(ngall, ngf.at[:, :, core], fs.at[3], fr.at[3], core_peer)
     outs = [
         pltpu.make_async_copy(ng_ref, ng_hbm, lsem.at[10]),
         pltpu.make_async_copy(nm_ref, nm_hbm, lsem.at[11]),
@@ -235,13 +237,45 @@
             )
             rs_copy[o, c, h].start()
 
+    half = tokens // 2
+    upper, lower = pl.ds(0, half), pl.ds(half, half)
+
+    def relay_partial(h):
+        for i, (o, rows) in enumerate(((1, upper), (3, lower))):
+            relayed[i, h] = remote(
+                psend.at[2, h, rows], held.at[i, h], hs.at[i, h], hr.at[i, h], x_peer(o)
+            )
+            relayed[i, h].start()
+        for o, rows in ((3, lower), (1, upper)):
+            rs_copy[o, 0, h] = remote(
+                psend.at[o, h, rows], precv.at[o, h, rows], rss.at[o, 0, h], rsr.at[o, 0, h], x_peer(NX - o)
+            )
+            rs_copy[o, 0, h].start()
+
+    def relay_sum(h):
+        for i, (o, rows) in enumerate(((3, upper), (1, lower))):
+            relayed[i, h].wait_recv()
+            psend[o, h, rows] = (psend[o, h, rows].astype(f32) + held[i, h].astype(f32)).astype(bf16)
+            relayed[2 + i, h] = remote(
+                psend.at[o, h, rows], precv.at[o, h, rows], hs.at[2 + i, h], hr.at[2 + i, h], x_peer(NX - o)
+            )
+            relayed[2 + i, h].start()
+
+    relayed = {}
+
     def key_gradient(c, h):
         first, size = pieces[c]
         rows = pl.ds(first, size)
         keys = kown[h, rows]
         for o in others:
-            rs_copy[o, c, h].wait_recv()
-            keys += precv[o, h, rows].astype(f32)
+            if (o, c, h) in rs_copy:
+                rs_copy[o, c, h].wait_recv()
+        if (2, h) in relayed:
+            relayed[2, h].wait_recv()
+            relayed[3, h].wait_recv()
+        for o in others:
+            if (o, c, h) in rs_copy:
+                keys += precv[o, h, rows].astype(f32)
         scale = lax.rsqrt(jnp.mean(keys * keys, axis=-1, keepdims=True) + norm_epsilon)
         normed = keys * scale
         upstream = ct[rows, columns(h)].astype(f32)
@@ -287,29 +321,32 @@
         average = gf_ref[...] - total / n_rep
         momentum_full = outer_beta * om_ref[...].astype(f32) + average
         global_new = gf_ref[...] - outer_rate * (average + outer_beta * momentum_full)
-        ngall[z] = global_new
-        each_z(lambda k: z_gather(k).start())
+        ngall[z, ylo] = global_new
+        ylo_back.start()
         ng_ref[...] = global_new
         nm_ref[...] = momentum_full.astype(bf16)
         for copy in outs:
             copy.start()
 
-    def ylo_return():
+    def gather_rows(first_plane):
+        def start():
+            ylo_back.wait_recv()
+            each_z(lambda k: z_gather(k).start())
+
+        if nz > 1:
+            pl.when(z == 0 if first_plane else z != 0)(start)
+        elif first_plane:
+            start()
+
+    def core_return():
         each_z(lambda k: z_gather(k).wait_recv())
-        back.append(remote(ngall, ng2.at[ylo], fs.at[2], fr.at[2], ylo_peer))
-        back[0].start()
-        ng2[ylo] = ngall[...]
-
-    def core_return():
-        back[0].wait_recv()
-        back.append(remote(ng2, ngf.at[:, :, core], fs.at[3], fr.at[3], core_peer))
-        back[1].start()
-        ngf[:, :, core] = ng2[...]
+        core_back.start()
+        ngf[:, :, core] = ngall[...]
 
     def all_left():
-        for copy in [w_copy, core_copy, ylo_copy, back[0]]:
+        for copy in [w_copy, core_copy, ylo_copy, ylo_back]:
             copy.wait_send()
-        for copies in (x_copy, rs_copy, ag_copy):
+        for copies in (x_copy, rs_copy, ag_copy, relayed):
             for copy in copies.values():
                 copy.wait_send()
         each_z(lambda k: z_sum(k).wait_send())
@@ -317,7 +354,7 @@
 
     def adam(h):
         if h == 0:
-            back[1].wait_recv()
+            core_back.wait_recv()
             loads[2].wait()
             loads[3].wait()
         time = jnp.full((1, HEAD), step_ref[0].astype(f32), f32)
@@ -335,7 +372,8 @@
             + weight_decay * weight
         )
         share = (1.0 - mix_share) * chosen[h]
-        updated = (1.0 - share) * updated + share * ngf[...].reshape(block, HEAD)
+        mixed = jnp.concatenate([ngf[:, i].reshape(block // 2, HEAD) for i in range(2)], axis=0)
+        updated = (1.0 - share) * updated + share * mixed
         wout[h] = updated.astype(bf16)
         fout[h] = first.astype(bf16)
         sout[h] = second.astype(bf16)
@@ -349,7 +387,7 @@
     loads[7].wait()
     steps = {
         "P": partial_keys, "R": send_partial, "K": key_gradient, "XT": turn, "G": send_gradient, "M": own_gradient,
-        "Z": outer_update, "YB": ylo_return, "CB": core_return, "L": all_left, "A": adam,
+        "Z": outer_update, "B": gather_rows, "T": relay_partial, "F": relay_sum, "CB": core_return, "L": all_left, "A": adam,
     }
     for name in ORDER:
         if name in steps:
@@ -357,7 +395,7 @@
         else:
             steps[name[0]](*map(int, name[1:]))
 
-    for copy in [back[1], *g_copy.values()]:
+    for copy in [core_back, *g_copy.values()]:
         copy.wait_send()
     for copy in outs:
         copy.wait()
@@ -424,9 +462,8 @@
                 pltpu.VMEM((nz, share, HEAD), f32),
                 pltpu.VMEM((nz, share, HEAD), f32),
                 pltpu.VMEM((nz, share, HEAD), f32),
-                pltpu.VMEM((nz, share, HEAD), f32),
-                pltpu.VMEM((2, nz, share, HEAD), f32),
-                pltpu.VMEM((2, nz, 2, share, HEAD), f32),
+                pltpu.VMEM((nz, 2, share, HEAD), f32),
+                pltpu.VMEM((nz, 2, 2, share, HEAD), f32),
                 dma((12,)),
                 dma((NX, len(PIECES), NY)), dma((NX, len(PIECES), NY)),
                 dma((1,)), dma((1,)),
@@ -437,6 +474,8 @@
                 dma((nz,)), dma((nz,)), dma((nz,)), dma((nz,)),
                 dma((3, KVH)),
                 *[pltpu.SemaphoreType.REGULAR] * 4,
+                pltpu.VMEM((2, KVH, tokens // 2, HEAD), bf16),
+                dma((4, KVH)), dma((4, KVH)),
             ],
             compiler_params=pltpu.CompilerParams(
                 collective_id=0, has_side_effects=True, vmem_limit_bytes=60 * 2**20

time: 60.9 us -> 62.9 us (1.033)
  the two profiles are of different devices: /device:TPU:16 before, /device:TPU:32 now
where the time goes in v4:
time: 62.9 us; the launch traced here: 62.7 us
  Pallas kernels  61.4 us (98%)
  between operations  1.29 us (2%)
    pallas_call x1, Pallas kernels, local(): pl.pallas_call(functools.partial(kernel, n_rep), out_shape=[jax.ShapeDtyp...  59.2 us
    pallas_call x1, Pallas kernels, local(): pl.pallas_call(writer, out_shape=[jax.ShapeDtypeStruct(r.shape, r.dtype)...  2.27 us

profile of v4, /device:TPU:32, one launch (start us, length us, event | category | flops | bytes accessed | tf_op | source)
XLA Modules:
  0.0 62.7 jit_solution(12328754210087050232)
XLA Ops:
  1.3 59.2 %shard_map.128 = (bf16[512,512]{1,0:T(8,128)(2,1)}, bf16[512,512]{1,0:T(8,128)(2,1)}, bf16[512,512]{1,0:T(8,128)(2,1)}, f32[8,128]{1,0:T(8,128)}, bf16[8,128]{1,0:T(8,128)(2,1)}) custom-call(bf16[192,4096]{1,0:T(8,128)(2,1)} %bitcast.8, bf16[512,512]{1,0:T(8,128)(2,1)} %bitcast.9, bf16[512,512]{1,0:T(8,128)(2,1)} %bitcast.10, bf16[512,512]{1,0:T(8,128)(2,1)} %bitcast.11, ...), custom_call_target="tpu_custom_call" | custom-call | tf_op jit(solution)/shard_map/pallas_call | solution.py:427
  60.5 2.3 %shard_map.129 = (bf16[512,512]{1,0:T(8,128)(2,1)}, bf16[512,512]{1,0:T(8,128)(2,1)}, bf16[512,512]{1,0:T(8,128)(2,1)}, f32[8,128]{1,0:T(8,128)}, bf16[8,128]{1,0:T(8,128)(2,1)}) custom-call(bf16[512,512]{1,0:T(8,128)(2,1)} %get-tuple-element.15.refs_0_, bf16[512,512]{1,0:T(8,128)(2,1)} %get-tuple-element.16.refs_1_, ...), custom_call_target="tpu_custom_call" | custom-call | tf_op jit(solution)/shard_map/pallas_call | solution.py:487

commit v5 on v4

--- a/solution.py
+++ b/solution.py
@@ -305,10 +305,12 @@
     def own_gradient(h):
         gown[h] = jnp.dot(xt[y], kgall[h], preferred_element_type=f32)
 
-    def outer_update(first_plane):
+    from_first = lax.rem(z + 2, nz)
+
+    def outer_update(early):
         if nz > 1:
-            pl.when(z == 0 if first_plane else z != 0)(outer_rows)
-        elif first_plane:
+            pl.when(from_first < 5 if early else from_first >= 5)(outer_rows)
+        elif early:
             outer_rows()
 
     def outer_rows():
@@ -328,14 +330,14 @@
         for copy in outs:
             copy.start()
 
-    def gather_rows(first_plane):
+    def gather_rows(early):
         def start():
             ylo_back.wait_recv()
             each_z(lambda k: z_gather(k).start())
 
         if nz > 1:
-            pl.when(z == 0 if first_plane else z != 0)(start)
-        elif first_plane:
+            pl.when(from_first < 5 if early else from_first >= 5)(start)
+        elif early:
             start()
 
     def core_return():

time: 62.9 us -> 61.1 us (0.971)
  the two profiles are of different devices: /device:TPU:32 before, /device:TPU:96 now
where the time goes in v5:
time: 61.1 us; the launch traced here: 61 us
  Pallas kernels  59.7 us (98%)
  between operations  1.29 us (2%)
    pallas_call x1, Pallas kernels, local(): pl.pallas_call(functools.partial(kernel, n_rep), out_shape=[jax.ShapeDtyp...  57.4 us
    pallas_call x1, Pallas kernels, local(): pl.pallas_call(writer, out_shape=[jax.ShapeDtypeStruct(r.shape, r.dtype)...  2.27 us

profile of v5, /device:TPU:96, one launch (start us, length us, event | category | flops | bytes accessed | tf_op | source)
XLA Modules:
  0.0 61.0 jit_solution(133392069211847235)
XLA Ops:
  1.3 57.4 %shard_map.128 = (bf16[512,512]{1,0:T(8,128)(2,1)}, bf16[512,512]{1,0:T(8,128)(2,1)}, bf16[512,512]{1,0:T(8,128)(2,1)}, f32[8,128]{1,0:T(8,128)}, bf16[8,128]{1,0:T(8,128)(2,1)}) custom-call(bf16[192,4096]{1,0:T(8,128)(2,1)} %bitcast.8, bf16[512,512]{1,0:T(8,128)(2,1)} %bitcast.9, bf16[512,512]{1,0:T(8,128)(2,1)} %bitcast.10, bf16[512,512]{1,0:T(8,128)(2,1)} %bitcast.11, ...), custom_call_target="tpu_custom_call" | custom-call | tf_op jit(solution)/shard_map/pallas_call | solution.py:429
  58.7 2.3 %shard_map.129 = (bf16[512,512]{1,0:T(8,128)(2,1)}, bf16[512,512]{1,0:T(8,128)(2,1)}, bf16[512,512]{1,0:T(8,128)(2,1)}, f32[8,128]{1,0:T(8,128)}, bf16[8,128]{1,0:T(8,128)(2,1)}) custom-call(bf16[512,512]{1,0:T(8,128)(2,1)} %get-tuple-element.15.refs_0_, bf16[512,512]{1,0:T(8,128)(2,1)} %get-tuple-element.16.refs_1_, ...), custom_call_target="tpu_custom_call" | custom-call | tf_op jit(solution)/shard_map/pallas_call | solution.py:489

commit v6 on v5

--- a/solution.py
+++ b/solution.py
@@ -25,7 +25,7 @@
 
 PIECES = (192,)
 ORDER = (
-    "P00", "R00", "T1", "P01", "T2", "T3", "Z0", "XT", "B0", "K00", "F1", "F2", "F3", "K01", "Z1", "K02",
+    "P00", "R00", "T1", "P01", "T2", "T3", "Z0", "XT", "K00", "F1", "F2", "F3", "B0", "K01", "Z1", "K02",
     "K03", "B1", "G0", "G1", "G2", "G3", "M0", "M1", "CB", "M2", "M3", "L", "A0", "A1", "A2", "A3",
 )
 MESH = pl.DeviceIdType.MESH

time: 61.1 us -> 60 us (0.982)
  the two profiles are of different devices: /device:TPU:96 before, /device:TPU:1 now
where the time goes in v6:
time: 60 us; the launch traced here: 59.4 us
  Pallas kernels  58.2 us (97%)
  between operations  1.29 us (2%)
    pallas_call x1, Pallas kernels, local(): pl.pallas_call(functools.partial(kernel, n_rep), out_shape=[jax.ShapeDtyp...  55.9 us
    pallas_call x1, Pallas kernels, local(): pl.pallas_call(writer, out_shape=[jax.ShapeDtypeStruct(r.shape, r.dtype)...  2.27 us

profile of v6, /device:TPU:1, one launch (start us, length us, event | category | flops | bytes accessed | tf_op | source)
XLA Modules:
  0.0 59.4 jit_solution(1491352708682613107)
XLA Ops:
  1.3 55.9 %shard_map.128 = (bf16[512,512]{1,0:T(8,128)(2,1)}, bf16[512,512]{1,0:T(8,128)(2,1)}, bf16[512,512]{1,0:T(8,128)(2,1)}, f32[8,128]{1,0:T(8,128)}, bf16[8,128]{1,0:T(8,128)(2,1)}) custom-call(bf16[192,4096]{1,0:T(8,128)(2,1)} %bitcast.8, bf16[512,512]{1,0:T(8,128)(2,1)} %bitcast.9, bf16[512,512]{1,0:T(8,128)(2,1)} %bitcast.10, bf16[512,512]{1,0:T(8,128)(2,1)} %bitcast.11, ...), custom_call_target="tpu_custom_call" | custom-call | tf_op jit(solution)/shard_map/pallas_call | solution.py:429
  57.2 2.3 %shard_map.129 = (bf16[512,512]{1,0:T(8,128)(2,1)}, bf16[512,512]{1,0:T(8,128)(2,1)}, bf16[512,512]{1,0:T(8,128)(2,1)}, f32[8,128]{1,0:T(8,128)}, bf16[8,128]{1,0:T(8,128)(2,1)}) custom-call(bf16[512,512]{1,0:T(8,128)(2,1)} %get-tuple-element.15.refs_0_, bf16[512,512]{1,0:T(8,128)(2,1)} %get-tuple-element.16.refs_1_, ...), custom_call_target="tpu_custom_call" | custom-call | tf_op jit(solution)/shard_map/pallas_call | solution.py:489

commit v7 on v6

--- a/solution.py
+++ b/solution.py
@@ -26,7 +26,7 @@
 PIECES = (192,)
 ORDER = (
     "P00", "R00", "T1", "P01", "T2", "T3", "Z0", "XT", "K00", "F1", "F2", "F3", "B0", "K01", "Z1", "K02",
-    "K03", "B1", "G0", "G1", "G2", "G3", "M0", "M1", "CB", "M2", "M3", "L", "A0", "A1", "A2", "A3",
+    "K03", "B1", "G0", "G1", "G2", "G3", "M0", "M1", "M2", "M3", "L", "CB", "A0", "A1", "A2", "A3",
 )
 MESH = pl.DeviceIdType.MESH
 f32 = jnp.float32
@@ -305,11 +305,11 @@
     def own_gradient(h):
         gown[h] = jnp.dot(xt[y], kgall[h], preferred_element_type=f32)
 
-    from_first = lax.rem(z + 2, nz)
+    from_first = lax.rem(z + 3, nz)
 
     def outer_update(early):
         if nz > 1:
-            pl.when(from_first < 5 if early else from_first >= 5)(outer_rows)
+            pl.when(from_first < 7 if early else from_first >= 7)(outer_rows)
         elif early:
             outer_rows()
 
@@ -336,7 +336,7 @@
             each_z(lambda k: z_gather(k).start())
 
         if nz > 1:
-            pl.when(from_first < 5 if early else from_first >= 5)(start)
+            pl.when(from_first < 7 if early else from_first >= 7)(start)
         elif early:
             start()
 

time: 60 us -> 59.8 us (level)
  no operation moved by 1% of the time
where the time goes in v7:
time: 59.8 us; the launch traced here: 59.6 us
  Pallas kernels  58.3 us (97%)
  between operations  1.29 us (2%)
    pallas_call x1, Pallas kernels, local(): pl.pallas_call(functools.partial(kernel, n_rep), out_shape=[jax.ShapeDtyp...  56.1 us
    pallas_call x1, Pallas kernels, local(): pl.pallas_call(writer, out_shape=[jax.ShapeDtypeStruct(r.shape, r.dtype)...  2.27 us

profile of v7, /device:TPU:1, one launch (start us, length us, event | category | flops | bytes accessed | tf_op | source)
XLA Modules:
  0.0 59.6 jit_solution(4167143972687865097)
XLA Ops:
  1.3 56.1 %shard_map.128 = (bf16[512,512]{1,0:T(8,128)(2,1)}, bf16[512,512]{1,0:T(8,128)(2,1)}, bf16[512,512]{1,0:T(8,128)(2,1)}, f32[8,128]{1,0:T(8,128)}, bf16[8,128]{1,0:T(8,128)(2,1)}) custom-call(bf16[192,4096]{1,0:T(8,128)(2,1)} %bitcast.8, bf16[512,512]{1,0:T(8,128)(2,1)} %bitcast.9, bf16[512,512]{1,0:T(8,128)(2,1)} %bitcast.10, bf16[512,512]{1,0:T(8,128)(2,1)} %bitcast.11, ...), custom_call_target="tpu_custom_call" | custom-call | tf_op jit(solution)/shard_map/pallas_call | solution.py:429
  57.3 2.3 %shard_map.129 = (bf16[512,512]{1,0:T(8,128)(2,1)}, bf16[512,512]{1,0:T(8,128)(2,1)}, bf16[512,512]{1,0:T(8,128)(2,1)}, f32[8,128]{1,0:T(8,128)}, bf16[8,128]{1,0:T(8,128)(2,1)}) custom-call(bf16[512,512]{1,0:T(8,128)(2,1)} %get-tuple-element.15.refs_0_, bf16[512,512]{1,0:T(8,128)(2,1)} %get-tuple-element.16.refs_1_, ...), custom_call_target="tpu_custom_call" | custom-call | tf_op jit(solution)/shard_map/pallas_call | solution.py:489
